TPU v7x, 32 devices: a whole 2x2x4 slice. The times are simulated.
32 devices in a mesh: groups: 2 (over y), batch: 8 (over z, x), mp: 2 (over core).
Axes of the slice: x: 2, y: 2, z: 4, core: 2. Of those that a mesh axis runs over, the one named last changes fastest.
Arguments:
- tokens: bfloat16 [1024, 16384], P(('groups', 'batch')), parts along dimension 0, may hold values from -6 to 6
- gate_weight: bfloat16 [16384, 256], P('batch', 'mp'), may hold values from -0.046875 to 0.046875
- up_weight: bfloat16 [16384, 256], P('batch', 'mp'), may hold values from -0.046875 to 0.046875
- down_weight: bfloat16 [256, 16384], P('mp', 'batch'), may hold values from -0.5 to 0.5
Outputs:
- mixed: bfloat16 [1024, 16384], P(('groups', 'batch'), 'mp'), parts along dimension 0
There are 2 independent parts, one for each index of `groups`. A program takes and returns all parts, laid end to end along the dimension named above; an argument that names none is the same for every part. Nothing has to cross between parts.
All inputs are finite; a program needn't handle non-finite values.
Results may differ from a plain program's by a relative error of at most 0.018.
Values may be sent and summed in bfloat16 or wider, within the bound.
A program may use at most 64 MiB of HBM per device.

v0:
```python
import jax
import jax.numpy as jnp
from jax import lax
from jax.sharding import PartitionSpec as P


def per_device(tokens, gate_weight, up_weight, down_weight):
    gate_sum = jnp.dot(
        tokens,
        lax.all_gather(gate_weight, "batch", axis=0, tiled=True),
        preferred_element_type=jnp.float32,
    )
    up_sum = jnp.dot(
        tokens,
        lax.all_gather(up_weight, "batch", axis=0, tiled=True),
        preferred_element_type=jnp.float32,
    )
    hidden = (jax.nn.silu(gate_sum) * up_sum).astype(jnp.bfloat16)
    partial_value = jnp.dot(
        hidden,
        lax.all_gather(down_weight, "batch", axis=1, tiled=True),
        preferred_element_type=jnp.float32,
    )
    return lax.psum_scatter(
        partial_value.astype(jnp.bfloat16), "mp", scatter_dimension=1, tiled=True
    )


def solution(mesh):
    return jax.shard_map(
        per_device,
        mesh=mesh,
        in_specs=(
            P(("groups", "batch"), None),
            P("batch", "mp"),
            P("batch", "mp"),
            P("mp", "batch"),
        ),
        out_specs=P(("groups", "batch"), "mp"),
        check_vma=False,
    )
```

profile of v0, /device:TPU:11, one launch (start us, length us, event | category | flops | bytes accessed | tf_op | source)
XLA Modules:
  0.0 253.4 jit_solution(9922367494734268384)
XLA Ops:
  6.5 0.0 copy-start
  6.5 0.0 all-gather.4.cloned.1.call-start
  6.5 0.7 all-gather.4.cloned.1.call-update
  7.3 0.0 all-gather.6.cloned.1.call-start
  7.3 0.7 all-gather.6.cloned.1.call-update
  8.0 0.0 all-gather.8.cloned.1.call-start
  8.1 0.7 all-gather.8.cloned.1.call-update
  8.7 0.0 reduce-scatter.2.cloned.1.call-start
  8.8 72.7 %all-gather.4.cloned.1.call-done = bf16[16384,128]{1,0:T(8,128)(2,1)} async-done(((bf16[2048,128]{1,0:T(8,128)(2,1)}), bf16[16384,128]{1,0:T(8,128)(2,1)}) %all-gather.4.cloned.1.call-update) | async-done | bytes 4194320 | tf_op jit(solution)/shard_map/all_gather | solution.py:10
  81.5 0.0 copy-done
  81.5 3.1 %fusion.8 = f32[64,128]{1,0:T(8,128)S(1)} fusion(bf16[64,16384]{1,0:T(8,128)(2,1)S(1)} %copy-done, bf16[16384,128]{1,0:T(8,128)(2,1)} %all-gather.4.cloned.1.call-done), kind=kOutput, calls=%fused_computation.10 | convolution fusion | flops 268435456 | bytes 6324224 | tf_op jit(solution)/shard_map/dot_general | solution.py:8
  84.5 70.7 %all-gather.6.cloned.1.call-done = bf16[16384,128]{1,0:T(8,128)(2,1)} async-done(((bf16[2048,128]{1,0:T(8,128)(2,1)}), bf16[16384,128]{1,0:T(8,128)(2,1)}) %all-gather.6.cloned.1.call-update) | async-done | bytes 4194320 | tf_op jit(solution)/shard_map/all_gather | solution.py:15
  155.3 73.9 %all-gather.8.cloned.1.call-done = bf16[128,16384]{1,0:T(8,128)(2,1)} async-done(((bf16[128,2048]{1,0:T(8,128)(2,1)}), bf16[128,16384]{1,0:T(8,128)(2,1)}) %all-gather.8.cloned.1.call-update) | async-done | bytes 4194320 | tf_op jit(solution)/shard_map/all_gather | solution.py:21
  229.1 6.3 %convolution_convert_fusion = bf16[64,16384]{1,0:T(8,128)(2,1)} fusion(bf16[128,16384]{1,0:T(8,128)(2,1)} %all-gather.8.cloned.1.call-done, bf16[64,16384]{1,0:T(8,128)(2,1)S(1)} %copy-done, bf16[16384,128]{1,0:T(8,128)(2,1)} %all-gather.6.cloned.1.call-done, f32[64,128]{1,0:T(8,128)S(1)} %fusion.8), kind=kOutput, calls=%fused_computation | convolution fusion | flops 537968640 | bytes 12615680 | tf_op jit(solution)/shard_map/dot_general | solution.py:19
  235.5 0.0 reduce-scatter.2.cloned.1.call-update
  235.5 11.3 %reduce-scatter.2.cloned.1.call-done = bf16[64,8192]{1,0:T(8,128)(2,1)} async-done(((bf16[64,16384]{1,0:T(8,128)(2,1)}), bf16[64,8192]{1,0:T(8,128)(2,1)}) %reduce-scatter.2.cloned.1.call-update) | async-done | bytes 1048592 | tf_op jit(solution)/shard_map/reduce_scatter | solution.py:24
Async XLA Ops:
  6.5 74.9 %copy-start = (bf16[64,16384]{1,0:T(8,128)(2,1)S(1)}, bf16[64,16384]{1,0:T(8,128)(2,1)}, u32[]{:S(2)}) copy-start(bf16[64,16384]{1,0:T(8,128)(2,1)} %param.4) | copy-start | bytes 6291460
  6.5 74.9 %all-gather.4.cloned.1.call-start = ((), (), s32[]{:S(2)}) async-start(), calls=%async_computation.1 | async-start | bytes 4718592 | tf_op jit(solution)/shard_map/all_gather | solution.py:10
  7.3 148.0 %all-gather.6.cloned.1.call-start = ((), (), s32[]{:S(2)}) async-start(), calls=%async_computation.2 | async-start | bytes 4718592 | tf_op jit(solution)/shard_map/all_gather | solution.py:15
  8.0 221.1 %all-gather.8.cloned.1.call-start = ((), (), s32[]{:S(2)}) async-start(), calls=%async_computation.3 | async-start | bytes 4718592 | tf_op jit(solution)/shard_map/all_gather | solution.py:21
  8.7 238.1 %reduce-scatter.2.cloned.1.call-start = ((), (), s32[]{:S(2)}) async-start(), calls=%async_computation.4 | async-start | bytes 3145728 | tf_op jit(solution)/shard_map/reduce_scatter | solution.py:24
Sparse Core Ops, SparseCore 0:
  9.5 71.9 all-gather.3
  83.6 71.6 all-gather.5
  157.5 71.6 all-gather.7
  235.6 11.1 reduce-scatter.1
where the time goes:
time: 254 us; the launch traced here: 253 us
  waiting for transfers between devices  231 us (91%)
  between operations  13.1 us (5%)
  matrix products  9.41 us (4%)
    all_gather x1, waiting for transfers between devices, per_device(): lax.all_gather(down_weight, 'batch', axis=1, tiled=True)  73.9 us
    all_gather x1, waiting for transfers between devices, per_device(): lax.all_gather(gate_weight, 'batch', axis=0, tiled=True)  72.7 us
    all_gather x1, waiting for transfers between devices, per_device(): lax.all_gather(up_weight, 'batch', axis=0, tiled=True)  70.7 us
    reduce_scatter x1, waiting for transfers between devices, per_device(): lax.psum_scatter(partial_value.astype(jnp.bfloat16), 'mp', scatter_dimens...  11.3 us
    dot_general x1, matrix products, per_device(): jnp.dot(hidden, lax.all_gather(down_weight, 'batch', axis=1, tiled=True),...  6.35 us
  transfers between devices with their start and end apart: 4, of which 4 were waited for; matrix products, arithmetic and copies ran while one was open for 1% of the time, Pallas kernels for 0%

commit v1 on v0

--- a/solution.py
+++ b/solution.py
@@ -1,10 +1,16 @@
+import functools
+
 import jax
 import jax.numpy as jnp
 from jax import lax
+from jax.experimental import pallas as pl
+from jax.experimental.pallas import tpu as pltpu
 from jax.sharding import PartitionSpec as P
 
-
-def per_device(tokens, gate_weight, up_weight, down_weight):
+MESH = pl.DeviceIdType.MESH
+
+
+def gathered(tokens, gate_weight, up_weight, down_weight):
     gate_sum = jnp.dot(
         tokens,
         lax.all_gather(gate_weight, "batch", axis=0, tiled=True),
@@ -26,9 +32,226 @@
     )
 
 
+def kernel(
+    nb, tok, gate_w, up_w, down_w, out,
+    wbuf, tbuf, dbuf, pbuf, rbuf, hsrc, hbuf, obuf,
+    loc_sem, wsend, wrecv, tsend, trecv, psend, precv, hsend, hrecv, osend, orecv,
+):
+    b, m = lax.axis_index("batch"), lax.axis_index("mp")
+    other = 1 - m
+    rows, width = tok.shape
+    half = rows // 2
+    depth, hid = gate_w.shape
+    cols = down_w.shape[1]
+    per_owner = nb // 2
+    owner, place = b // per_owner, b % per_owner
+
+    def at(index, size):
+        return pl.ds(pl.multiple_of(index * size, size), size)
+
+    def peer(i):
+        return lax.rem(b + i, nb)
+
+    def remote(src, dst, send, recv, chip, core):
+        return pltpu.make_async_remote_copy(
+            src_ref=src, dst_ref=dst, send_sem=send, recv_sem=recv,
+            device_id={"batch": chip, "mp": core}, device_id_type=MESH,
+        )
+
+    def swap(k):
+        src, dst = [
+            (gate_w, wbuf.at[:, at(m, hid)]),
+            (up_w, wbuf.at[:, at(2 + m, hid)]),
+            (down_w, dbuf.at[at(m, hid), :]),
+        ][k]
+        return src, dst
+
+    def token_copy(i):
+        chip = peer(i)
+        return remote(
+            tok.at[at(m, half), at(chip, depth)], tbuf.at[at(b, half), :],
+            tsend.at[chip], trecv.at[b], chip, m,
+        )
+
+    def partial_copy(chip):
+        return remote(pbuf.at[chip], rbuf.at[b], psend.at[chip], precv.at[b], chip, m)
+
+    def hidden_copy(i):
+        chip = peer(i)
+        return remote(hsrc, hbuf.at[at(b, half), :], hsend.at[chip], hrecv.at[b], chip, m)
+
+    slot = place * 2 + m
+
+    def out_dst():
+        return out.at[at(m, half), at(place, cols)]
+
+    def out_copy(chip):
+        return remote(
+            obuf.at[at(chip, half), :], out_dst(), osend.at[chip], orecv.at[slot], chip, owner
+        )
+
+    local = [pltpu.make_async_copy(*swap(k), loc_sem.at[k]) for k in range(3)]
+    local.append(
+        pltpu.make_async_copy(
+            tok.at[at(m, half), at(b, depth)], tbuf.at[at(b, half), :], loc_sem.at[3]
+        )
+    )
+    for copy in local:
+        copy.start()
+
+    barrier = pltpu.get_barrier_semaphore()
+    for i in range(nb):
+        for j in range(2):
+            if i or j:
+                pl.semaphore_signal(
+                    barrier, inc=1,
+                    device_id={"batch": peer(i), "mp": lax.rem(m + j, 2)},
+                    device_id_type=MESH,
+                )
+    pl.semaphore_wait(barrier, 2 * nb - 1)
+
+    for i in range(1, nb):
+        token_copy(i).start()
+    swaps = []
+    for k in range(3):
+        src, dst = swap(k)
+        swaps.append(remote(src, dst, wsend.at[k], wrecv.at[k], b, other))
+        swaps[-1].start()
+    for copy in local:
+        copy.wait()
+    for k in range(2):
+        swaps[k].wait_recv()
+
+    z, x = b // 2, b % 2
+
+    def first(step, carry):
+        pair = lax.rem(z + step, nb // 2)
+        for j in range(2):
+            chip = pair * 2 + j
+
+            @pl.when(chip != b)
+            def _():
+                remote(
+                    tok.at[at(m, half), at(chip, depth)], tbuf.at[at(chip, half), :],
+                    tsend.at[chip], trecv.at[chip], chip, m,
+                ).wait_recv()
+
+        sums = jnp.dot(
+            tbuf[at(pair, rows), :], wbuf[...], preferred_element_type=jnp.float32
+        ).astype(jnp.bfloat16)
+        for j in range(2):
+            chip = pair * 2 + j
+            pbuf[chip] = sums[j * half : (j + 1) * half]
+
+            @pl.when(chip != b)
+            def _():
+                partial_copy(chip).start()
+
+        return carry
+
+    lax.fori_loop(0, nb // 2, first, 0)
+
+    total = pbuf[b].astype(jnp.float32)
+    for i in range(1, nb):
+        chip = peer(i)
+        remote(
+            pbuf.at[chip], rbuf.at[chip], psend.at[chip], precv.at[chip], chip, m
+        ).wait_recv()
+        total += rbuf[chip].astype(jnp.float32)
+    gate, up = total[:, : 2 * hid], total[:, 2 * hid :]
+    hidden = (gate / (1.0 + jnp.exp(-gate)) * up).astype(jnp.bfloat16)
+    hsrc[...] = hidden
+    for i in range(1, nb):
+        hidden_copy(i).start()
+    hbuf[at(b, half), :] = hidden
+    swaps[2].wait_recv()
+
+    def second(step, carry):
+        pair = lax.rem(z + step, nb // 2)
+        for j in range(2):
+            chip = pair * 2 + j
+
+            @pl.when(chip != b)
+            def _():
+                remote(
+                    hsrc, hbuf.at[at(chip, half), :], hsend.at[chip], hrecv.at[chip], chip, m
+                ).wait_recv()
+
+        obuf[at(pair, rows), :] = jnp.dot(
+            hbuf[at(pair, rows), :], dbuf[...], preferred_element_type=jnp.float32
+        ).astype(jnp.bfloat16)
+        for j in range(2):
+            chip = pair * 2 + j
+            here = jnp.logical_and(chip == b, owner == m)
+
+            @pl.when(jnp.logical_not(here))
+            def _():
+                out_copy(chip).start()
+
+            @pl.when(here)
+            def _():
+                pltpu.make_async_copy(
+                    obuf.at[at(chip, half), :], out_dst(), orecv.at[slot]
+                ).start()
+
+        return carry
+
+    lax.fori_loop(0, nb // 2, second, 0)
+
+    for i in range(1, nb):
+        token_copy(i).wait_send()
+        partial_copy(peer(i)).wait_send()
+        hidden_copy(i).wait_send()
+        out_copy(peer(i)).wait_send()
+    for copy in swaps:
+        copy.wait_send()
+
+    @pl.when(owner != m)
+    def _():
+        out_copy(b).wait_send()
+
+    for k in range(per_owner):
+        for j in range(2):
+            pltpu.make_async_copy(
+                obuf.at[pl.ds(0, half), :],
+                out.at[pl.ds(j * half, half), pl.ds(k * cols, cols)],
+                orecv.at[k * 2 + j],
+            ).wait()
+
+
+def exchanged(nb, tokens, gate_weight, up_weight, down_weight):
+    rows, width = tokens.shape
+    half = rows // 2
+    depth, hid = gate_weight.shape
+    cols = down_weight.shape[1]
+    bf16 = jnp.bfloat16
+    sems = [4, 3, 3] + [nb] * 8
+    return pl.pallas_call(
+        functools.partial(kernel, nb),
+        out_shape=jax.ShapeDtypeStruct((rows, width // 2), bf16),
+        in_specs=[pl.BlockSpec(memory_space=pl.ANY)] * 4,
+        out_specs=pl.BlockSpec(memory_space=pl.ANY),
+        scratch_shapes=[
+            pltpu.VMEM((depth, 4 * hid), bf16),
+            pltpu.VMEM((nb * half, depth), bf16),
+            pltpu.VMEM((2 * hid, cols), bf16),
+            pltpu.VMEM((nb, half, 4 * hid), bf16),
+            pltpu.VMEM((nb, half, 4 * hid), bf16),
+            pltpu.VMEM((half, 2 * hid), bf16),
+            pltpu.VMEM((nb * half, 2 * hid), bf16),
+            pltpu.VMEM((nb * half, cols), bf16),
+        ] + [pltpu.SemaphoreType.DMA((n,)) for n in sems],
+        compiler_params=pltpu.CompilerParams(
+            collective_id=0, has_side_effects=True, vmem_limit_bytes=40 * 2**20
+        ),
+    )(tokens, gate_weight, up_weight, down_weight)
+
+
 def solution(mesh):
+    nb = mesh.shape["batch"]
+    small = mesh.shape["mp"] == 2 and nb % 2 == 0
     return jax.shard_map(
-        per_device,
+        functools.partial(exchanged, nb) if small else gathered,
         mesh=mesh,
         in_specs=(
             P(("groups", "batch"), None),

time: 254 us -> 69.7 us (0.27)
  waiting for transfers between devices: 231 us -> 0 us
  Pallas kernels: 0 us -> 63.7 us
  between operations: 13.1 us -> 0.01 us
  matrix products: 9.41 us -> 0 us
  local copies, waits for them, and re-layouts: 0.01 us -> 5.69 us
    all_gather x3 -> x0, waiting for transfers between devices: 217 us -> none  [the longest x1 73.9 us: per_device(): lax.all_gather(down_weight, 'batch', axis=1, tiled=True)]
    pallas_call x0 -> x1, Pallas kernels: none -> 63.7 us  [exchanged(): pl.pallas_call(functools.partial(kernel, nb), out_shape=jax.ShapeDtypeStr...]
    reduce_scatter x1 -> x0, waiting for transfers between devices: 11.3 us -> none  [per_device(): lax.psum_scatter(partial_value.astype(jnp.bfloat16), 'mp', scatter_dimens...]
    dot_general x2 -> x0, matrix products: 9.41 us -> none  [the longest x1 6.35 us: per_device(): jnp.dot(hidden, lax.all_gather(down_weight, 'batch', axis=1, tiled=True),...]
    unnamed x2 -> x9, local copies, waits for them, and re-layouts: 0.01 us -> 5.69 us
  transfers between devices with their start and end apart: 4 -> 0, of which waited for: 4 -> 0; matrix products, arithmetic and copies ran while one was open for 1% -> 0% of each run, Pallas kernels for 0% -> 0%
where the time goes in v1:
time: 69.7 us; the launch traced here: 69.4 us
  Pallas kernels  63.7 us (91%)
  local copies, waits for them, and re-layouts  5.69 us (8%)
    pallas_call x1, Pallas kernels, exchanged(): pl.pallas_call(functools.partial(kernel, nb), out_shape=jax.ShapeDtypeStr...  63.7 us
    unnamed x9, local copies, waits for them, and re-layouts  5.69 us

profile of v1, /device:TPU:11, one launch (start us, length us, event | category | flops | bytes accessed | tf_op | source)
XLA Modules:
  0.0 69.4 jit_solution(8496243121607551699)
XLA Ops:
  0.0 0.0 copy-start
  0.0 1.6 %copy-done = bf16[64,16384]{1,0:T(8,128)(2,1)S(1)} copy-done((bf16[64,16384]{1,0:T(8,128)(2,1)S(1)}, bf16[64,16384]{1,0:T(8,128)(2,1)}, u32[]{:S(2)}) %copy-start) | copy-done | bytes 2097176
  1.6 0.0 copy-start.1
  1.6 1.0 %copy-done.1 = bf16[2048,128]{1,0:T(8,128)(2,1)S(1)} copy-done((bf16[2048,128]{1,0:T(8,128)(2,1)S(1)}, bf16[2048,128]{1,0:T(8,128)(2,1)}, u32[]{:S(2)}) %copy-start.1) | copy-done | bytes 524312
  2.6 0.0 copy-start.2
  2.6 1.0 %copy-done.2 = bf16[2048,128]{1,0:T(8,128)(2,1)S(1)} copy-done((bf16[2048,128]{1,0:T(8,128)(2,1)S(1)}, bf16[2048,128]{1,0:T(8,128)(2,1)}, u32[]{:S(2)}) %copy-start.2) | copy-done | bytes 524312
  3.7 0.0 copy-start.3
  3.7 1.0 %copy-done.3 = bf16[128,2048]{1,0:T(8,128)(2,1)S(1)} copy-done((bf16[128,2048]{1,0:T(8,128)(2,1)S(1)}, bf16[128,2048]{1,0:T(8,128)(2,1)}, u32[]{:S(2)}) %copy-start.3) | copy-done | bytes 524312
  4.7 63.7 %shard_map.46 = bf16[64,8192]{1,0:T(8,128)(2,1)S(1)} custom-call(bf16[64,16384]{1,0:T(8,128)(2,1)S(1)} %copy-done, bf16[2048,128]{1,0:T(8,128)(2,1)S(1)} %copy-done.1, bf16[2048,128]{1,0:T(8,128)(2,1)S(1)} %copy-done.2, bf16[128,2048]{1,0:T(8,128)(2,1)S(1)} %copy-done.3), custom_call_target="tpu_custom_call" | custom-call | tf_op jit(solution)/shard_map/pallas_call | solution.py:229
  68.5 1.0 %copy.6 = bf16[64,8192]{1,0:T(8,128)(2,1)} copy(bf16[64,8192]{1,0:T(8,128)(2,1)S(1)} %shard_map.46) | data formatting | bytes 2097152
Async XLA Ops:
  0.0 1.6 %copy-start = (bf16[64,16384]{1,0:T(8,128)(2,1)S(1)}, bf16[64,16384]{1,0:T(8,128)(2,1)}, u32[]{:S(2)}) copy-start(bf16[64,16384]{1,0:T(8,128)(2,1)} %tok.1) | copy-start | bytes 6291460
  1.6 1.0 %copy-start.1 = (bf16[2048,128]{1,0:T(8,128)(2,1)S(1)}, bf16[2048,128]{1,0:T(8,128)(2,1)}, u32[]{:S(2)}) copy-start(bf16[2048,128]{1,0:T(8,128)(2,1)} %gate_w.1) | copy-start | bytes 1572868
  2.6 1.0 %copy-start.2 = (bf16[2048,128]{1,0:T(8,128)(2,1)S(1)}, bf16[2048,128]{1,0:T(8,128)(2,1)}, u32[]{:S(2)}) copy-start(bf16[2048,128]{1,0:T(8,128)(2,1)} %up_w.1) | copy-start | bytes 1572868
  3.7 1.0 %copy-start.3 = (bf16[128,2048]{1,0:T(8,128)(2,1)S(1)}, bf16[128,2048]{1,0:T(8,128)(2,1)}, u32[]{:S(2)}) copy-start(bf16[128,2048]{1,0:T(8,128)(2,1)} %down_w.1) | copy-start | bytes 1572868

commit v2 on v0

--- a/solution.py
+++ b/solution.py
@@ -1,10 +1,16 @@
+import functools
+
 import jax
 import jax.numpy as jnp
 from jax import lax
+from jax.experimental import pallas as pl
+from jax.experimental.pallas import tpu as pltpu
 from jax.sharding import PartitionSpec as P
 
-
-def per_device(tokens, gate_weight, up_weight, down_weight):
+MESH = pl.DeviceIdType.MESH
+
+
+def gathered(tokens, gate_weight, up_weight, down_weight):
     gate_sum = jnp.dot(
         tokens,
         lax.all_gather(gate_weight, "batch", axis=0, tiled=True),
@@ -26,9 +32,253 @@
     )
 
 
+def kernel(
+    nb, parts, tok, gate_w, up_w, down_w, out,
+    wbuf, tbuf, dbuf, pbuf, rbuf, hsrc, hbuf, obuf,
+    loc_sem, wsend, wrecv, tsend, trecv, psend, precv, hsend, hrecv, osend, orecv,
+):
+    b, m = lax.axis_index("batch"), lax.axis_index("mp")
+    other = 1 - m
+    rows = tok.shape[0]
+    half = rows // 2
+    size = half // parts
+    depth, hid = gate_w.shape
+    cols = down_w.shape[1]
+    nz = nb // 2
+    z, x = b // 2, b % 2
+    across = 2 * z + 1 - x
+    per_owner = nz // 2
+    owner, place = z // per_owner, z % per_owner
+
+    def at(index, extent):
+        return pl.ds(pl.multiple_of(index * extent, extent), extent)
+
+    def remote(src, dst, send, recv, chip, core):
+        return pltpu.make_async_remote_copy(
+            src_ref=src, dst_ref=dst, send_sem=send, recv_sem=recv,
+            device_id={"batch": chip, "mp": core}, device_id_type=MESH,
+        )
+
+    def mine(c):
+        return pl.ds(pl.multiple_of(m * half + c * size, size), size)
+
+    def token_copy(c, chip, source):
+        return remote(
+            tok.at[mine(c), at(chip, depth)], tbuf.at[at(c * nb + source, size), :],
+            tsend.at[c * nb + chip], trecv.at[c * nb + source], chip, m,
+        )
+
+    def partial_copy(c, chip, source):
+        return remote(
+            pbuf.at[c * nb + chip], rbuf.at[c * nb + source],
+            psend.at[c * nb + chip], precv.at[c * nb + source], chip, m,
+        )
+
+    def hidden_copy(c, zone, source):
+        return remote(
+            hsrc.at[c], hbuf.at[at(c * nz + source, size), :],
+            hsend.at[c * nz + zone], hrecv.at[c * nz + source], 2 * zone + x, m,
+        )
+
+    def slot(c):
+        return (c * per_owner + place) * 2 + m
+
+    def out_dst(c):
+        return out.at[mine(c), at(place, 2 * cols)]
+
+    def out_src(c, zone):
+        return obuf.at[at(c * nz + zone, size), :]
+
+    def out_copy(c, zone):
+        return remote(
+            out_src(c, zone), out_dst(c), osend.at[c * nz + zone], orecv.at[slot(c)],
+            2 * zone + x, owner,
+        )
+
+    own_down = dbuf.at[at(m, hid), at(x, cols)]
+    swapped = [
+        (gate_w, wbuf.at[:, at(m, hid)]),
+        (up_w, wbuf.at[:, at(2 + m, hid)]),
+        (down_w, own_down),
+    ]
+    local = [pltpu.make_async_copy(*pair, loc_sem.at[k]) for k, pair in enumerate(swapped)]
+    for c in range(parts):
+        local.append(
+            pltpu.make_async_copy(
+                tok.at[mine(c), at(b, depth)], tbuf.at[at(c * nb + b, size), :],
+                loc_sem.at[3 + c],
+            )
+        )
+    for copy in local:
+        copy.start()
+
+    barrier = pltpu.get_barrier_semaphore()
+    for i in range(nb):
+        for j in range(2):
+            if i or j:
+                pl.semaphore_signal(
+                    barrier, inc=1,
+                    device_id={"batch": lax.rem(b + i, nb), "mp": lax.rem(m + j, 2)},
+                    device_id_type=MESH,
+                )
+    pl.semaphore_wait(barrier, 2 * nb - 1)
+
+    swaps = [
+        remote(src, dst, wsend.at[k], wrecv.at[k], b, other)
+        for k, (src, dst) in enumerate(swapped)
+    ]
+    over = remote(down_w, own_down, wsend.at[3], wrecv.at[3], across, m)
+    got = dbuf.at[at(m, hid), at(1 - x, cols)]
+    onward = remote(got, got, wsend.at[4], wrecv.at[4], b, other)
+
+    for i in range(1, nb):
+        token_copy(0, lax.rem(b + i, nb), b).start()
+    swaps[0].start()
+    swaps[1].start()
+    for c in range(1, parts):
+        for i in range(1, nb):
+            token_copy(c, lax.rem(b + i, nb), b).start()
+    swaps[2].start()
+    over.start()
+    for copy in local:
+        copy.wait()
+    swaps[0].wait_recv()
+    swaps[1].wait_recv()
+
+    def first(c):
+        def pair_of_chips(step, carry):
+            zone = lax.rem(z + step, nz)
+            for j in range(2):
+                chip = zone * 2 + j
+
+                @pl.when(chip != b)
+                def _():
+                    token_copy(c, chip, chip).wait_recv()
+
+            sums = jnp.dot(
+                tbuf[at(c * nz + zone, 2 * size), :], wbuf[...],
+                preferred_element_type=jnp.float32,
+            ).astype(jnp.bfloat16)
+            for j in range(2):
+                chip = zone * 2 + j
+                pbuf[c * nb + chip] = sums[j * size : (j + 1) * size]
+
+                @pl.when(chip != b)
+                def _():
+                    partial_copy(c, chip, b).start()
+
+            return carry
+
+        lax.fori_loop(0, nz, pair_of_chips, 0)
+
+    def reduce(c):
+        total = pbuf[c * nb + b].astype(jnp.float32)
+        for i in range(1, nb):
+            chip = lax.rem(b + i, nb)
+            partial_copy(c, chip, chip).wait_recv()
+            total += rbuf[c * nb + chip].astype(jnp.float32)
+        gate, up = total[:, : 2 * hid], total[:, 2 * hid :]
+        hidden = (gate / (1.0 + jnp.exp(-gate)) * up).astype(jnp.bfloat16)
+        hsrc[c] = hidden
+        for i in range(1, nz):
+            hidden_copy(c, lax.rem(z + i, nz), z).start()
+        hbuf[at(c * nz + z, size), :] = hidden
+
+    def second(c):
+        for i in range(1, nz):
+            zone = lax.rem(z + i, nz)
+            hidden_copy(c, zone, zone).wait_recv()
+        obuf[c * nz * size : (c + 1) * nz * size, :] = jnp.dot(
+            hbuf[c * nz * size : (c + 1) * nz * size, :], dbuf[...],
+            preferred_element_type=jnp.float32,
+        ).astype(jnp.bfloat16)
+        for i in range(1, nz):
+            out_copy(c, lax.rem(z + i, nz)).start()
+
+        @pl.when(owner != m)
+        def _():
+            out_copy(c, z).start()
+
+        @pl.when(owner == m)
+        def _():
+            pltpu.make_async_copy(out_src(c, z), out_dst(c), orecv.at[slot(c)]).start()
+
+    first(0)
+    over_in = remote(got, got, wsend.at[3], wrecv.at[3], across, m)
+    over_in.wait_recv()
+    onward.start()
+    for c in range(parts):
+        reduce(c)
+        if c + 1 < parts:
+            first(c + 1)
+        if c == 0:
+            swaps[2].wait_recv()
+            onward.wait_recv()
+        second(c)
+
+    for c in range(parts):
+        for i in range(1, nb):
+            chip = lax.rem(b + i, nb)
+            token_copy(c, chip, b).wait_send()
+            partial_copy(c, chip, b).wait_send()
+        for i in range(1, nz):
+            zone = lax.rem(z + i, nz)
+            hidden_copy(c, zone, z).wait_send()
+            out_copy(c, zone).wait_send()
+
+        @pl.when(owner != m)
+        def _():
+            out_copy(c, z).wait_send()
+
+    for copy in swaps + [over, onward]:
+        copy.wait_send()
+
+    for c in range(parts):
+        for k in range(per_owner):
+            for j in range(2):
+                pltpu.make_async_copy(
+                    obuf.at[pl.ds(0, size), :],
+                    out.at[pl.ds(j * half + c * size, size), pl.ds(k * 2 * cols, 2 * cols)],
+                    orecv.at[(c * per_owner + k) * 2 + j],
+                ).wait()
+
+
+def exchanged(nb, tokens, gate_weight, up_weight, down_weight):
+    rows, width = tokens.shape
+    half = rows // 2
+    parts = 2
+    size = half // parts
+    depth, hid = gate_weight.shape
+    cols = down_weight.shape[1]
+    nz = nb // 2
+    bf16 = jnp.bfloat16
+    sems = [3 + parts, 5, 5] + [parts * nb] * 4 + [parts * nz] * 4
+    return pl.pallas_call(
+        functools.partial(kernel, nb, parts),
+        out_shape=jax.ShapeDtypeStruct((rows, width // 2), bf16),
+        in_specs=[pl.BlockSpec(memory_space=pltpu.HBM)] * 4,
+        out_specs=pl.BlockSpec(memory_space=pltpu.HBM),
+        scratch_shapes=[
+            pltpu.VMEM((depth, 4 * hid), bf16),
+            pltpu.VMEM((nb * half, depth), bf16),
+            pltpu.VMEM((2 * hid, 2 * cols), bf16),
+            pltpu.VMEM((parts * nb, size, 4 * hid), bf16),
+            pltpu.VMEM((parts * nb, size, 4 * hid), bf16),
+            pltpu.VMEM((parts, size, 2 * hid), bf16),
+            pltpu.VMEM((nz * half, 2 * hid), bf16),
+            pltpu.VMEM((nz * half, 2 * cols), bf16),
+        ] + [pltpu.SemaphoreType.DMA((n,)) for n in sems],
+        compiler_params=pltpu.CompilerParams(
+            collective_id=0, has_side_effects=True, vmem_limit_bytes=40 * 2**20
+        ),
+    )(tokens, gate_weight, up_weight, down_weight)
+
+
 def solution(mesh):
+    nb = mesh.shape["batch"]
+    small = mesh.shape["mp"] == 2 and nb % 4 == 0
     return jax.shard_map(
-        per_device,
+        functools.partial(exchanged, nb) if small else gathered,
         mesh=mesh,
         in_specs=(
             P(("groups", "batch"), None),

time: 254 us -> 67.7 us (0.27)
  waiting for transfers between devices: 231 us -> 0 us
  Pallas kernels: 0 us -> 61.6 us
  between operations: 13.1 us -> 0.01 us
  matrix products: 9.41 us -> 0 us
  local copies, waits for them, and re-layouts: 0.01 us -> 5.69 us
    all_gather x3 -> x0, waiting for transfers between devices: 217 us -> none  [the longest x1 73.9 us: per_device(): lax.all_gather(down_weight, 'batch', axis=1, tiled=True)]
    pallas_call x0 -> x1, Pallas kernels: none -> 61.6 us  [exchanged(): pl.pallas_call(functools.partial(kernel, nb, parts), out_shape=jax.ShapeD...]
    reduce_scatter x1 -> x0, waiting for transfers between devices: 11.3 us -> none  [per_device(): lax.psum_scatter(partial_value.astype(jnp.bfloat16), 'mp', scatter_dimens...]
    dot_general x2 -> x0, matrix products: 9.41 us -> none  [the longest x1 6.35 us: per_device(): jnp.dot(hidden, lax.all_gather(down_weight, 'batch', axis=1, tiled=True),...]
    unnamed x2 -> x9, local copies, waits for them, and re-layouts: 0.01 us -> 5.69 us
  transfers between devices with their start and end apart: 4 -> 0, of which waited for: 4 -> 0; matrix products, arithmetic and copies ran while one was open for 1% -> 0% of each run, Pallas kernels for 0% -> 0%
where the time goes in v2:
time: 67.7 us; the launch traced here: 67.3 us
  Pallas kernels  61.6 us (91%)
  local copies, waits for them, and re-layouts  5.69 us (8%)
    pallas_call x1, Pallas kernels, exchanged(): pl.pallas_call(functools.partial(kernel, nb, parts), out_shape=jax.ShapeD...  61.6 us
    unnamed x9, local copies, waits for them, and re-layouts  5.69 us

profile of v2, /device:TPU:11, one launch (start us, length us, event | category | flops | bytes accessed | tf_op | source)
XLA Modules:
  0.0 67.3 jit_solution(8851488290541831107)
XLA Ops:
  0.0 0.0 copy-start
  0.0 1.6 %copy-done = bf16[64,16384]{1,0:T(8,128)(2,1)S(1)} copy-done((bf16[64,16384]{1,0:T(8,128)(2,1)S(1)}, bf16[64,16384]{1,0:T(8,128)(2,1)}, u32[]{:S(2)}) %copy-start) | copy-done | bytes 2097176
  1.6 0.0 copy-start.1
  1.6 1.0 %copy-done.1 = bf16[2048,128]{1,0:T(8,128)(2,1)S(1)} copy-done((bf16[2048,128]{1,0:T(8,128)(2,1)S(1)}, bf16[2048,128]{1,0:T(8,128)(2,1)}, u32[]{:S(2)}) %copy-start.1) | copy-done | bytes 524312
  2.6 0.0 copy-start.2
  2.6 1.0 %copy-done.2 = bf16[2048,128]{1,0:T(8,128)(2,1)S(1)} copy-done((bf16[2048,128]{1,0:T(8,128)(2,1)S(1)}, bf16[2048,128]{1,0:T(8,128)(2,1)}, u32[]{:S(2)}) %copy-start.2) | copy-done | bytes 524312
  3.7 0.0 copy-start.3
  3.7 1.0 %copy-done.3 = bf16[128,2048]{1,0:T(8,128)(2,1)S(1)} copy-done((bf16[128,2048]{1,0:T(8,128)(2,1)S(1)}, bf16[128,2048]{1,0:T(8,128)(2,1)}, u32[]{:S(2)}) %copy-start.3) | copy-done | bytes 524312
  4.7 61.6 %shard_map.46 = bf16[64,8192]{1,0:T(8,128)(2,1)S(1)} custom-call(bf16[64,16384]{1,0:T(8,128)(2,1)S(1)} %copy-done, bf16[2048,128]{1,0:T(8,128)(2,1)S(1)} %copy-done.1, bf16[2048,128]{1,0:T(8,128)(2,1)S(1)} %copy-done.2, bf16[128,2048]{1,0:T(8,128)(2,1)S(1)} %copy-done.3), custom_call_target="tpu_custom_call" | custom-call | tf_op jit(solution)/shard_map/pallas_call | solution.py:256
  66.3 1.0 %copy.6 = bf16[64,8192]{1,0:T(8,128)(2,1)} copy(bf16[64,8192]{1,0:T(8,128)(2,1)S(1)} %shard_map.46) | data formatting | bytes 2097152
Async XLA Ops:
  0.0 1.6 %copy-start = (bf16[64,16384]{1,0:T(8,128)(2,1)S(1)}, bf16[64,16384]{1,0:T(8,128)(2,1)}, u32[]{:S(2)}) copy-start(bf16[64,16384]{1,0:T(8,128)(2,1)} %tok.1) | copy-start | bytes 6291460
  1.6 1.0 %copy-start.1 = (bf16[2048,128]{1,0:T(8,128)(2,1)S(1)}, bf16[2048,128]{1,0:T(8,128)(2,1)}, u32[]{:S(2)}) copy-start(bf16[2048,128]{1,0:T(8,128)(2,1)} %gate_w.1) | copy-start | bytes 1572868
  2.6 1.0 %copy-start.2 = (bf16[2048,128]{1,0:T(8,128)(2,1)S(1)}, bf16[2048,128]{1,0:T(8,128)(2,1)}, u32[]{:S(2)}) copy-start(bf16[2048,128]{1,0:T(8,128)(2,1)} %up_w.1) | copy-start | bytes 1572868
  3.7 1.0 %copy-start.3 = (bf16[128,2048]{1,0:T(8,128)(2,1)S(1)}, bf16[128,2048]{1,0:T(8,128)(2,1)}, u32[]{:S(2)}) copy-start(bf16[128,2048]{1,0:T(8,128)(2,1)} %down_w.1) | copy-start | bytes 1572868

commit v3 on v2

--- a/solution.py
+++ b/solution.py
@@ -147,7 +147,7 @@
 
     def first(c):
         def pair_of_chips(step, carry):
-            zone = lax.rem(z + step, nz)
+            zone = lax.rem(z + nz - step, nz)
             for j in range(2):
                 chip = zone * 2 + j
 
@@ -174,7 +174,7 @@
     def reduce(c):
         total = pbuf[c * nb + b].astype(jnp.float32)
         for i in range(1, nb):
-            chip = lax.rem(b + i, nb)
+            chip = lax.rem(b + nb - i, nb)
             partial_copy(c, chip, chip).wait_recv()
             total += rbuf[c * nb + chip].astype(jnp.float32)
         gate, up = total[:, : 2 * hid], total[:, 2 * hid :]
@@ -207,13 +207,12 @@
     over_in = remote(got, got, wsend.at[3], wrecv.at[3], across, m)
     over_in.wait_recv()
     onward.start()
+    for c in range(1, parts):
+        first(c)
+    swaps[2].wait_recv()
+    onward.wait_recv()
     for c in range(parts):
         reduce(c)
-        if c + 1 < parts:
-            first(c + 1)
-        if c == 0:
-            swaps[2].wait_recv()
-            onward.wait_recv()
         second(c)
 
     for c in range(parts):
@@ -269,7 +268,7 @@
             pltpu.VMEM((nz * half, 2 * cols), bf16),
         ] + [pltpu.SemaphoreType.DMA((n,)) for n in sems],
         compiler_params=pltpu.CompilerParams(
-            collective_id=0, has_side_effects=True, vmem_limit_bytes=40 * 2**20
+            collective_id=0, has_side_effects=True, vmem_limit_bytes=60 * 2**20
         ),
     )(tokens, gate_weight, up_weight, down_weight)
 

time: 67.7 us -> 63.4 us (0.936)
  local copies, waits for them, and re-layouts: 5.69 us -> 2.26 us
  Pallas kernels: 61.6 us -> 60.3 us
    unnamed x9 -> x1, local copies, waits for them, and re-layouts: 5.69 us -> 2.26 us
    pallas_call x1, Pallas kernels: 61.6 us -> 60.3 us  [exchanged(): pl.pallas_call(functools.partial(kernel, nb, parts), out_shape=jax.ShapeD...]
where the time goes in v3:
time: 63.4 us; the launch traced here: 62.6 us
  Pallas kernels  60.3 us (95%)
  local copies, waits for them, and re-layouts  2.26 us (4%)
    pallas_call x1, Pallas kernels, exchanged(): pl.pallas_call(functools.partial(kernel, nb, parts), out_shape=jax.ShapeD...  60.3 us
    unnamed x1, local copies, waits for them, and re-layouts  2.26 us

profile of v3, /device:TPU:11, one launch (start us, length us, event | category | flops | bytes accessed | tf_op | source)
XLA Modules:
  0.0 62.6 jit_solution(3556307658189525570)
XLA Ops:
  0.0 60.3 %shard_map.46 = bf16[64,8192]{1,0:T(8,128)(2,1)} custom-call(bf16[64,16384]{1,0:T(8,128)(2,1)} %tok.1, bf16[2048,128]{1,0:T(8,128)(2,1)} %gate_w.1, bf16[2048,128]{1,0:T(8,128)(2,1)} %up_w.1, bf16[128,2048]{1,0:T(8,128)(2,1)} %down_w.1), custom_call_target="tpu_custom_call" | custom-call | tf_op jit(solution)/shard_map/pallas_call | solution.py:255
  60.3 2.3 %copy.6 = bf16[64,8192]{1,0:T(8,128)(2,1)} copy(bf16[64,8192]{1,0:T(8,128)(2,1)} %shard_map.46) | data formatting | bytes 2097152

commit v4 on v3

--- a/solution.py
+++ b/solution.py
@@ -136,7 +136,7 @@
     swaps[0].start()
     swaps[1].start()
     for c in range(1, parts):
-        for i in range(1, nb):
+        for i in range(1, 4):
             token_copy(c, lax.rem(b + i, nb), b).start()
     swaps[2].start()
     over.start()
@@ -145,7 +145,7 @@
     swaps[0].wait_recv()
     swaps[1].wait_recv()
 
-    def first(c):
+    def first(c, low=0, high=nb // 2):
         def pair_of_chips(step, carry):
             zone = lax.rem(z + nz - step, nz)
             for j in range(2):
@@ -169,7 +169,7 @@
 
             return carry
 
-        lax.fori_loop(0, nz, pair_of_chips, 0)
+        lax.fori_loop(low, high, pair_of_chips, 0)
 
     def reduce(c):
         total = pbuf[c * nb + b].astype(jnp.float32)
@@ -204,16 +204,20 @@
             pltpu.make_async_copy(out_src(c, z), out_dst(c), orecv.at[slot(c)]).start()
 
     first(0)
+    for c in range(1, parts):
+        for i in range(4, nb):
+            token_copy(c, lax.rem(b + i, nb), b).start()
     over_in = remote(got, got, wsend.at[3], wrecv.at[3], across, m)
     over_in.wait_recv()
     onward.start()
-    for c in range(1, parts):
-        first(c)
+    first(1, 0, 1)
+    reduce(0)
+    first(1, 1, nz)
     swaps[2].wait_recv()
     onward.wait_recv()
-    for c in range(parts):
-        reduce(c)
-        second(c)
+    second(0)
+    reduce(1)
+    second(1)
 
     for c in range(parts):
         for i in range(1, nb):

time: 63.4 us -> 62.8 us (level)
  no operation moved by 1% of the time
where the time goes in v4:
time: 62.8 us; the launch traced here: 62.1 us
  Pallas kernels  59.8 us (95%)
  local copies, waits for them, and re-layouts  2.26 us (4%)
    pallas_call x1, Pallas kernels, exchanged(): pl.pallas_call(functools.partial(kernel, nb, parts), out_shape=jax.ShapeD...  59.8 us
    unnamed x1, local copies, waits for them, and re-layouts  2.26 us

profile of v4, /device:TPU:11, one launch (start us, length us, event | category | flops | bytes accessed | tf_op | source)
XLA Modules:
  0.0 62.1 jit_solution(3708755392146438491)
XLA Ops:
  0.0 59.8 %shard_map.46 = bf16[64,8192]{1,0:T(8,128)(2,1)} custom-call(bf16[64,16384]{1,0:T(8,128)(2,1)} %tok.1, bf16[2048,128]{1,0:T(8,128)(2,1)} %gate_w.1, bf16[2048,128]{1,0:T(8,128)(2,1)} %up_w.1, bf16[128,2048]{1,0:T(8,128)(2,1)} %down_w.1), custom_call_target="tpu_custom_call" | custom-call | tf_op jit(solution)/shard_map/pallas_call | solution.py:259
  59.8 2.3 %copy.6 = bf16[64,8192]{1,0:T(8,128)(2,1)} copy(bf16[64,8192]{1,0:T(8,128)(2,1)} %shard_map.46) | data formatting | bytes 2097152
